TPU v7x, 32 devices: a whole 2x2x4 slice. The times are simulated.
32 devices in a mesh: dp: 8 (over z, x), head: 4 (over y, core).
Axes of the slice: x: 2, y: 2, z: 4, core: 2. Of those that a mesh axis runs over, the one named last changes fastest.
Arguments:
- layer_input: bfloat16 [256, 250, 128], P('dp'), may hold values from -6 to 6
- cotangent: bfloat16 [256, 250, 128], P('dp'), may hold values from -6 to 6
- window_count: int32 [8], P('dp'), may hold values from 1 to 32, as said below
- sample_weight: float32 [256], P('dp'), may hold values from 0.3 to 3
- ln1_gain: float32 [2, 128], replicated, may hold values from 0.5 to 1.5
- ln1_shift: float32 [2, 128], replicated, may hold values from -2 to 2
- qkv_weight: bfloat16 [2, 128, 384], P(None, None, 'head'), may hold values from -0.5 to 0.5
- qv_bias: float32 [2, 256], P(None, 'head'), may hold values from -3 to 3
- out_weight: bfloat16 [2, 128, 128], replicated, may hold values from -3 to 3
- out_bias: float32 [2, 128], replicated, may hold values from -2 to 2
- ln2_gain: float32 [2, 128], replicated, may hold values from 0.5 to 1.5
- ln2_shift: float32 [2, 128], replicated, may hold values from -2 to 2
- up_weight: bfloat16 [2, 128, 512], replicated, may hold values from -0.5 to 0.5
- up_bias: float32 [2, 512], replicated, may hold values from -3 to 3
- down_weight: bfloat16 [2, 512, 128], replicated, may hold values from -0.25 to 0.25
- down_bias: float32 [2, 128], replicated, may hold values from -2 to 2
Outputs:
- layer_out: bfloat16 [256, 250, 128], P('dp', None, 'head')
- input_grad: float32 [256, 250, 128], P('dp', None, 'head')
- ln1_gain_grad: float32 [2, 128], replicated
- ln1_shift_grad: float32 [2, 128], replicated
- qkv_weight_grad: float32 [2, 128, 384], P(None, None, 'head')
- qv_bias_grad: float32 [2, 256], P(None, 'head')
- out_weight_grad: float32 [2, 128, 128], P(None, 'head')
- out_bias_grad: float32 [2, 128], replicated
- ln2_gain_grad: float32 [2, 128], replicated
- ln2_shift_grad: float32 [2, 128], replicated
- up_weight_grad: float32 [2, 128, 512], P(None, None, 'head')
- up_bias_grad: float32 [2, 512], P(None, 'head')
- down_weight_grad: float32 [2, 512, 128], P(None, 'head')
- down_bias_grad: float32 [2, 128], replicated
Inputs may be any that keep to these rules, and one draw needn't show every extreme that they name: The first window_count slots of each dp index hold real windows, the others are padding; some dp index has all 32 slots real.
All inputs are finite; a program needn't handle non-finite values.
Results may differ from a plain program's by a relative error of at most 0.019.
Values may be sent and summed in bfloat16 or wider, within the bound.
A program may use at most 384 MiB of HBM per device.

v0:
```python
import math

import jax
import jax.numpy as jnp
from jax import lax
from jax.sharding import PartitionSpec as P

norm_eps = 1e-05
window_group = 4
inv_root_two = 0.7071067811865476
inv_root_tau = 0.3989422804014327


def contract_rows(left_arr, right_arr):
    return lax.dot_general(
        left_arr, right_arr, (((0,), (0,)), ((), ())), preferred_element_type=jnp.float32
    )


def contract_cols(left_arr, right_arr):
    return lax.dot_general(
        left_arr, right_arr, (((1,), (1,)), ((), ())), preferred_element_type=jnp.float32
    )


def normalize(values, gain, shift):
    center = values - jnp.mean(values, axis=-1, keepdims=True)
    spread_inv = lax.rsqrt(jnp.mean(center * center, axis=-1, keepdims=True) + norm_eps)
    unit_vals = center * spread_inv
    return (unit_vals * gain + shift, unit_vals, spread_inv)


def norm_backward(grad_norm, gain, unit_vals, spread_inv):
    scaled = grad_norm * gain
    return spread_inv * (
        scaled
        - jnp.mean(scaled, axis=-1, keepdims=True)
        - unit_vals * jnp.mean(scaled * unit_vals, axis=-1, keepdims=True)
    )


def gelu_slope(pre):
    return (
        0.5 * (1.0 + lax.erf(pre * inv_root_two)) + pre * jnp.exp(-0.5 * pre * pre) * inv_root_tau
    )


def causal_mask(window_len):
    return lax.broadcasted_iota(jnp.int32, (window_len, window_len), 0) >= lax.broadcasted_iota(
        jnp.int32, (window_len, window_len), 1
    )


def head_forward(block):
    queries, key_rows, value_rows = block
    window_len = queries.shape[1]
    score_scale = 1.0 / math.sqrt(queries.shape[2])
    scores = (
        jnp.einsum("gqd,gkd->gqk", queries, key_rows, preferred_element_type=jnp.float32)
        * score_scale
    )
    scores = jnp.where(causal_mask(window_len), scores, -1e30)
    row_top = jnp.max(scores, axis=-1, keepdims=True)
    expo = jnp.exp(scores - row_top)
    totals = jnp.sum(expo, axis=-1, keepdims=True)
    probs_low = (expo / totals).astype(jnp.bfloat16)
    output = jnp.einsum("gqk,gkd->gqd", probs_low, value_rows, preferred_element_type=jnp.float32)
    log_total = row_top[..., 0] + jnp.log(totals[..., 0])
    return (output.astype(jnp.bfloat16), log_total)


def head_backward(block):
    queries, key_rows, value_rows, log_total, grad_out = block
    window_len = queries.shape[1]
    score_scale = 1.0 / math.sqrt(queries.shape[2])
    scores = (
        jnp.einsum("gqd,gkd->gqk", queries, key_rows, preferred_element_type=jnp.float32)
        * score_scale
    )
    scores = jnp.where(causal_mask(window_len), scores, -1e30)
    probs = jnp.exp(scores - log_total[..., None])
    probs_low = probs.astype(jnp.bfloat16)
    grad_probs = jnp.einsum(
        "gqd,gkd->gqk", grad_out, value_rows, preferred_element_type=jnp.float32
    )
    grad_values = jnp.einsum(
        "gqk,gqd->gkd", probs_low, grad_out, preferred_element_type=jnp.float32
    )
    row_dot = jnp.sum(grad_probs * probs, axis=-1, keepdims=True)
    grad_scores = (probs * (grad_probs - row_dot)).astype(jnp.bfloat16)
    grad_queries = (
        jnp.einsum("gqk,gkd->gqd", grad_scores, key_rows, preferred_element_type=jnp.float32)
        * score_scale
    )
    grad_keys = (
        jnp.einsum("gqk,gqd->gkd", grad_scores, queries, preferred_element_type=jnp.float32)
        * score_scale
    )
    return (grad_queries, grad_keys, grad_values)


def split_heads(qkv_rows, head_dim, slot_count, window_len):
    shaped = qkv_rows.reshape(slot_count // window_group, window_group, window_len, 3 * head_dim)
    return (
        shaped[..., :head_dim],
        shaped[..., head_dim : 2 * head_dim],
        shaped[..., 2 * head_dim :],
    )


def run_layer(stream, params, slot_count, window_len):
    (
        gain_one,
        shift_one,
        qkv_w,
        qv_b,
        out_w,
        out_b,
        gain_two,
        shift_two,
        up_w,
        up_b,
        down_w,
        down_b,
    ) = params
    row_count = stream.shape[0]
    head_dim = qkv_w.shape[1] // 3
    norm_one, unit_one, spread_one = normalize(stream, gain_one, shift_one)
    norm_one_low = norm_one.astype(jnp.bfloat16)
    bias_pair = qv_b.reshape(2, head_dim)
    bias_full = jnp.concatenate([bias_pair[0], jnp.zeros((head_dim,), jnp.float32), bias_pair[1]])
    qkv_rows = (
        jnp.dot(norm_one_low, qkv_w, preferred_element_type=jnp.float32) + bias_full
    ).astype(jnp.bfloat16)
    attended, log_total = lax.map(
        head_forward, split_heads(qkv_rows, head_dim, slot_count, window_len)
    )
    attended = attended.reshape(row_count, head_dim)
    projected = jnp.dot(
        lax.all_gather(attended, "head", axis=1, tiled=True),
        out_w,
        preferred_element_type=jnp.float32,
    )
    mixed = stream + projected + out_b
    norm_two, unit_two, spread_two = normalize(mixed, gain_two, shift_two)
    norm_two_low = norm_two.astype(jnp.bfloat16)
    pre = jnp.dot(norm_two_low, up_w, preferred_element_type=jnp.float32) + up_b
    act = jax.nn.gelu(pre, approximate=False).astype(jnp.bfloat16)
    result = mixed + jnp.dot(act, down_w, preferred_element_type=jnp.float32) + down_b
    saved = (
        unit_one,
        spread_one,
        norm_one_low,
        qkv_rows,
        log_total,
        attended,
        unit_two,
        spread_two,
        norm_two_low,
        pre,
        act,
    )
    return (result, saved)


def shards(
    layer_input,
    cotangent,
    window_count,
    sample_weight,
    ln1_gain,
    ln1_shift,
    qkv_weight,
    qv_bias,
    out_weight,
    out_bias,
    ln2_gain,
    ln2_shift,
    up_weight,
    up_bias,
    down_weight,
    down_bias,
):
    slot_count, window_len, model_width = layer_input.shape
    head_count = lax.axis_size("head")
    own_head = lax.axis_index("head")
    head_dim = model_width // head_count
    layer_count = ln1_gain.shape[0]
    hidden_units = up_weight.shape[2]
    unit_share = hidden_units // head_count
    row_count = slot_count * window_len

    def layer_params(layer_idx):
        return tuple(
            (
                param[layer_idx]
                for param in (
                    ln1_gain,
                    ln1_shift,
                    qkv_weight,
                    qv_bias,
                    out_weight,
                    out_bias,
                    ln2_gain,
                    ln2_shift,
                    up_weight,
                    up_bias,
                    down_weight,
                    down_bias,
                )
            )
        )

    stream = layer_input.astype(jnp.float32).reshape(row_count, model_width)
    inputs_kept = []
    saved_kept = []
    for layer_idx in range(layer_count):
        inputs_kept.append(stream)
        stream, saved = run_layer(stream, layer_params(layer_idx), slot_count, window_len)
        saved_kept.append(saved)
    feature_start = own_head * head_dim
    layer_out = (
        lax.dynamic_slice_in_dim(stream, feature_start, head_dim, 1)
        .astype(jnp.bfloat16)
        .reshape(slot_count, window_len, head_dim)
    )
    valid = (lax.broadcasted_iota(jnp.int32, (slot_count,), 0) < window_count[0]).astype(
        jnp.float32
    )
    weights = sample_weight * valid
    grad_z = (cotangent.astype(jnp.float32) * weights[:, None, None]).reshape(
        row_count, model_width
    )
    collected = [None] * layer_count
    for layer_idx in reversed(range(layer_count)):
        params = layer_params(layer_idx)
        (
            gain_one,
            shift_one,
            qkv_w,
            qv_b,
            out_w,
            out_b,
            gain_two,
            shift_two,
            up_w,
            up_b,
            down_w,
            down_b,
        ) = params
        _, saved = run_layer(inputs_kept[layer_idx], params, slot_count, window_len)
        (
            unit_one,
            spread_one,
            norm_one_low,
            qkv_rows,
            log_total,
            attended,
            unit_two,
            spread_two,
            norm_two_low,
            pre,
            act,
        ) = saved
        unit_start = own_head * unit_share
        grad_low = grad_z.astype(jnp.bfloat16)
        down_bias_part = jnp.sum(grad_low.astype(jnp.float32), axis=0)
        act_own = lax.dynamic_slice_in_dim(act, unit_start, unit_share, 1)
        down_weight_part = contract_rows(act_own, grad_low)
        down_own = lax.dynamic_slice_in_dim(down_w, unit_start, unit_share, 0)
        pre_own = lax.dynamic_slice_in_dim(pre, unit_start, unit_share, 1)
        grad_pre = (contract_cols(grad_low, down_own) * gelu_slope(pre_own)).astype(jnp.bfloat16)
        up_own = lax.dynamic_slice_in_dim(up_w, unit_start, unit_share, 1)
        grad_norm_two = contract_cols(grad_pre, up_own)
        partial_back = norm_backward(grad_norm_two, gain_two, unit_two, spread_two)
        back_two, gain_two_part, shift_two_part = (
            lax.psum(partial_back.astype(jnp.bfloat16), "head").astype(jnp.float32),
            lax.psum(jnp.sum(grad_norm_two * unit_two, axis=0).astype(jnp.bfloat16), "head").astype(
                jnp.float32
            ),
            lax.psum(jnp.sum(grad_norm_two, axis=0).astype(jnp.bfloat16), "head").astype(
                jnp.float32
            ),
        )
        up_weight_part = contract_rows(norm_two_low, grad_pre)
        up_bias_part = jnp.sum(grad_pre.astype(jnp.float32), axis=0)
        grad_mixed = grad_z + back_two
        grad_mixed_low = grad_mixed.astype(jnp.bfloat16)
        out_bias_part = jnp.sum(grad_mixed_low.astype(jnp.float32), axis=0)
        out_weight_part = contract_rows(attended, grad_mixed_low)
        out_own = lax.dynamic_slice_in_dim(out_w, feature_start, head_dim, 0)
        grad_attended = contract_cols(grad_mixed_low, out_own).astype(jnp.bfloat16)
        queries, key_rows, value_rows = split_heads(qkv_rows, head_dim, slot_count, window_len)
        grad_shaped = grad_attended.reshape(
            slot_count // window_group, window_group, window_len, head_dim
        )
        grad_queries, grad_keys, grad_values = lax.map(
            head_backward, (queries, key_rows, value_rows, log_total, grad_shaped)
        )
        grad_qkv = (
            jnp.concatenate([grad_queries, grad_keys, grad_values], axis=-1)
            .reshape(row_count, 3 * head_dim)
            .astype(jnp.bfloat16)
        )
        qkv_weight_part = contract_rows(norm_one_low, grad_qkv)
        grad_qkv_sums = jnp.sum(grad_qkv.astype(jnp.float32), axis=0)
        qv_bias_part = jnp.concatenate([grad_qkv_sums[:head_dim], grad_qkv_sums[2 * head_dim :]])
        grad_norm_one = contract_cols(grad_qkv, qkv_w)
        gain_one_part = jnp.sum(grad_norm_one * unit_one, axis=0)
        shift_one_part = jnp.sum(grad_norm_one, axis=0)
        head_term = norm_backward(grad_norm_one, gain_one, unit_one, spread_one) + grad_mixed * (
            1.0 / head_count
        )
        if layer_idx == 0:
            grad_z = lax.psum_scatter(
                head_term.astype(jnp.bfloat16), "head", scatter_dimension=1, tiled=True
            ).astype(jnp.float32)
        else:
            grad_z = lax.psum(head_term.astype(jnp.bfloat16), "head").astype(jnp.float32)
        collected[layer_idx] = (
            gain_one_part,
            shift_one_part,
            qkv_weight_part,
            qv_bias_part,
            out_weight_part,
            out_bias_part,
            gain_two_part,
            shift_two_part,
            up_weight_part,
            up_bias_part,
            down_weight_part,
            down_bias_part,
        )
    stacked = [
        jnp.stack([collected[layer_idx][member] for layer_idx in range(layer_count)])
        for member in range(12)
    ]
    summed = lax.psum(
        (
            stacked[2],
            stacked[3],
            stacked[4],
            stacked[5],
            stacked[6],
            stacked[7],
            stacked[8],
            stacked[9],
            stacked[10],
            stacked[11],
        ),
        "dp",
    )
    norm_sums = lax.psum((stacked[0], stacked[1]), ("dp", "head"))
    input_grad = grad_z.reshape(slot_count, window_len, head_dim)
    return (
        layer_out,
        input_grad,
        norm_sums[0],
        norm_sums[1],
        summed[0],
        summed[1],
        summed[2],
        summed[3],
        summed[4],
        summed[5],
        summed[6],
        summed[7],
        summed[8],
        summed[9],
    )


def solution(mesh):
    return jax.shard_map(
        shards,
        mesh=mesh,
        in_specs=(
            P("dp", None, None),
            P("dp", None, None),
            P("dp"),
            P("dp"),
            P(),
            P(),
            P(None, None, "head"),
            P(None, "head"),
            P(),
            P(),
            P(),
            P(),
            P(),
            P(),
            P(),
            P(),
        ),
        out_specs=(
            P("dp", None, "head"),
            P("dp", None, "head"),
            P(),
            P(),
            P(None, None, "head"),
            P(None, "head"),
            P(None, "head", None),
            P(),
            P(),
            P(),
            P(None, None, "head"),
            P(None, "head"),
            P(None, "head", None),
            P(),
        ),
        check_vma=False,
    )
```

profile of v0, /device:TPU:0, one launch (start us, length us, event | category | flops | bytes accessed | tf_op | source)
XLA Modules:
  0.0 956.9 jit_solution(17813228888525245448)
XLA Ops:
  28.8 7.2 reshape.320
  40.8 19.6 %while.74 = (s32[]{:T(128)}, bf16[8,4,250,32]{2,1,0,3:T(4,128)(2,1)}, f32[8,4,250]{2,1,0:T(4,128)S(1)}, bf16[8,4,250,32]{2,3,1,0:T(8,128)(2,1)S(1)}, bf16[8,4,25...) while((s32[]{:T(128)}, bf16[8,4,250,32]{2,1,0,3:T(4,128)(2,1)}, ...), condition=%wide.region_19.20_spmd, body=%wide.region_16.19_spmd.sunk | while | flops 34093500 | bytes 3551589 | solution.py:135
  64.4 22.8 %while.72 = (s32[]{:T(128)}, bf16[8,4,250,32]{2,1,0,3:T(4,128)(2,1)}, bf16[8,4,250,32]{2,3,1,0:T(8,128)(2,1)S(1)}, bf16[8,4,250,32]{2,3,1,0:T(8,128)(2,1)S(1)}, bf16[8,4,250,32]{2,3,1,0:T(8,128)(2,1)}, /*index=5*/s32[]{:T(128)}) while((s32[]{:T(128)}, bf16[8,4,250,32]{2,1,0,3:T(4,128)(2,1)}, bf16[8,4,250,32]{2,3,1,0:T(8,128)(2,1)S(1)}, ...), condition=%wide.region_5.6_spmd, body=%wide.region_2.5_spmd.sunk | while | flops 50345996 | bytes 725525 | solution.py:135
  108.8 6.5 copy.161
  144.1 52.8 %fusion.400 = (f32[8000]{0:T(1024)S(1)}, f32[8000,128]{0,1:T(8,128)}) fusion(f32[128]{0:T(128)S(1)} %get-tuple-element.521, f32[8000,128]{0,1:T(8,128)} %copy-done.19, bf16[2,512,128]{2,1,0:T(8,128)(2,1)S(1)} %copy-done.48, f32[512]{0:T(512)S(1)} %bitcast.506, f32[128]{0:T(128)S(1)} %get-tuple-element.525, f32[128]{0:T(128)S(1)} %get-tuple-element.568, ...), kind=kOutput, calls=%fused_computation.536 | convolution fusion | flops 2375672064 | bytes 12716800 | tf_op jit(solution)/shard_map/dot_general | solution.py:149
  204.1 7.2 reshape.322
  216.1 19.6 %while.75 = (s32[]{:T(128)}, bf16[8,4,250,32]{2,1,0,3:T(4,128)(2,1)}, f32[8,4,250]{2,1,0:T(4,128)S(1)}, bf16[8,4,250,32]{2,3,1,0:T(8,128)(2,1)S(1)}, bf16[8,4,25...) while((s32[]{:T(128)}, bf16[8,4,250,32]{2,1,0,3:T(4,128)(2,1)}, ...), condition=%wide.region_23.24_spmd, body=%wide.region_20.0_spmd.sunk | while | flops 34093500 | bytes 3551589 | solution.py:135
  238.5 35.0 %negate_multiply_fusion.1 = (f32[8000,512]{1,0:T(8,128)}, f32[8000,512]{1,0:T(8,128)}, f32[8000,512]{1,0:T(8,128)}, f32[8000,512]{1,0:T(8,128)}, f32[8000,512]{1,0:T(8,128)}) fusion(f32[512]{0:T(512)S(1)} %bitcast.507, bf16[8000,128]{0,1:T(8,128)(2,1)S(1)} %add_convert_fusion.1, bf16[2,128,512]{2,1,0:T(8,128)(2,1)} %param.40), kind=kOutput, calls=%fused_computation.175 | convolution fusion | flops 1265664000 | bytes 84101120 | tf_op jit(solution)/shard_map/dot_general | solution.py:147
  273.7 18.1 %while.73 = (s32[]{:T(128)}, bf16[8,4,250,32]{2,1,0,3:T(4,128)(2,1)S(1)}, bf16[8,4,250,32]{2,3,1,0:T(8,128)(2,1)S(1)}, bf16[8,4,250,32]{2,3,1,0:T(8,128)(2,1)S(1)}, bf16[8,4,250,32]{2,3,1,0:T(8,128)(2,1)}, /*index=5*/s32[]{:T(128)}) while((s32[]{:T(128)}, bf16[8,4,250,32]{2,1,0,3:T(4,128)(2,1)S(1)}, bf16[8,4,250,32]{2,3,1,0:T(8,128)(2,1)S(1)}, ...), condition=%wide.region_13.14_spmd, body=%wide.region_10.13_spmd.sunk | while | flops 50345996 | bytes 727061 | solution.py:135
  293.4 9.4 negate_compare_fusion.1
  309.2 9.4 all-gather.7.cloned.1.call-done
  326.7 43.0 %fusion.205 = f32[8000,128]{0,1:T(8,128)} fusion(f32[512]{0:T(512)S(1)} %bitcast.504, f32[8000,128]{0,1:T(8,128)} %copy-done.16, f32[128]{0:T(128)S(1)} %copy-done.69, f32[128]{0:T(128)S(1)} %copy-done.62, f32[8000]{0:T(1024)S(1)} %add_rsqrt_fusion.2, f32[8000]{0:T(1024)S(1)} %broadcast_multiply_fusion.10, bf16[2,512,128]{2,1,0:T(8,128)(2,1)S(1)} %copy-done.48, ...), kind=kOutput, calls=%fused_computation.305 | convolution fusion | flops 2372608000 | bytes 8522752 | tf_op jit(solution)/shard_map/dot_general | solution.py:149
  369.6 33.5 %negate_multiply_fusion = (f32[8000,512]{1,0:T(8,128)}, f32[8000,512]{1,0:T(8,128)}, f32[8000,512]{1,0:T(8,128)}, f32[8000,512]{1,0:T(8,128)}, f32[8000,512]{1,0:T(8,128)}) fusion(f32[512]{0:T(512)S(1)} %bitcast.505, bf16[8000,128]{0,1:T(8,128)(2,1)S(1)} %add_convert_fusion.3, bf16[2,128,512]{2,1,0:T(8,128)(2,1)S(1)} %copy-done.50), kind=kOutput, calls=%fused_computation.172 | convolution fusion | flops 1265664000 | bytes 84117504 | tf_op jit(solution)/shard_map/dot_general | solution.py:147
  424.6 10.0 %negate_compare_fusion = pred[8000,512]{1,0:T(32,128)(4,1)} fusion(f32[8000,512]{1,0:T(8,128)} %get-tuple-element.556), kind=kLoop, calls=%fused_computation.206 | loop fusion | flops 20480000 | bytes 20480000 | tf_op jit(solution)/shard_map/erfc | solution.py:148
  434.6 41.0 %all-reduce.9.cloned.1.call-done = bf16[8000,128]{0,1:T(8,128)(2,1)} async-done(((bf16[8000,128]{0,1:T(8,128)(2,1)}), bf16[8000,128]{0,1:T(8,128)(2,1)}) %all-reduce.9.cloned.1.call-update) | async-done | bytes 2048016 | tf_op jit(solution)/shard_map/psum | solution.py:277
  484.8 58.5 %while.76 = (s32[]{:T(128)}, bf16[8,4,250,32]{2,3,1,0:T(8,128)(2,1)}, bf16[8,4,250,32]{2,3,1,0:T(8,128)(2,1)S(1)}, bf16[8,4,250,32]{2,3,1,0:T(8,128)(2,1)S(1)}, ...) while((s32[]{:T(128)}, ...), condition=%wide.region_31.32_spmd, body=%wide.region_29.31_spmd.sunk | while | flops 82375504 | bytes 8699493 | solution.py:297
  588.5 40.6 %all-reduce.11.cloned.1.call-done = bf16[8000,128]{0,1:T(8,128)(2,1)} async-done(((bf16[8000,128]{0,1:T(8,128)(2,1)}), bf16[8000,128]{0,1:T(8,128)(2,1)}) %all-reduce.11.cloned.1.call-update) | async-done | bytes 2048016 | tf_op jit(solution)/shard_map/psum | solution.py:319
  651.5 11.2 %fusion.237 = f32[1,128,128]{2,1,0:T(8,128)S(1)} fusion(f32[8000,128]{1,0:T(8,128)} %reshape.325, f32[8000,512]{1,0:T(8,128)} %get-tuple-element.503, s32[]{:T(128)S(6)} %select_n.35, f32[8000,512]{1,0:T(8,128)} %get-tuple-element.502, f32[8000,512]{1,0:T(8,128)} %get-tuple-element.501, pred[8000,512]{1,0:T(32,128)(4,1)} %negate_compare_fusion, ...), kind=kOutput, calls=%fused_computation.325 | convolution fusion | flops 275456000 | bytes 25665540 | tf_op jit(solution)/shard_map/dot_general | solution.py:15
  670.0 32.3 %all-reduce.13.cloned.1.call-done = bf16[8000,128]{0,1:T(8,128)(2,1)} async-done(((bf16[8000,128]{0,1:T(8,128)(2,1)}), bf16[8000,128]{0,1:T(8,128)(2,1)}) %all-reduce.13.cloned.1.call-update) | async-done | bytes 2048016 | tf_op jit(solution)/shard_map/psum | solution.py:277
  708.1 58.4 %while.77 = (s32[]{:T(128)}, bf16[8,4,250,32]{2,3,1,0:T(8,128)(2,1)}, bf16[8,4,250,32]{2,3,1,0:T(8,128)(2,1)S(1)}, bf16[8,4,250,32]{2,3,1,0:T(8,128)(2,1)S(1)}, ...) while((s32[]{:T(128)}, ...), condition=%wide.region_42.43_spmd, body=%wide.region_40.42_spmd.sunk | while | flops 82375504 | bytes 8699493 | solution.py:297
  816.7 9.7 %fusion.234 = f32[1,128,128]{2,1,0:T(8,128)S(1)} fusion(bf16[8000,128]{0,1:T(8,128)(2,1)S(1)} %copy-done.13, f32[8000,512]{1,0:T(8,128)} %get-tuple-element.499, s32[]{:T(128)S(6)} %select_n.35, f32[8000,512]{1,0:T(8,128)} %get-tuple-element.498, f32[8000,512]{1,0:T(8,128)} %get-tuple-element.497, pred[8000,512]{1,0:T(32,128)(4,1)} %negate_compare_fusion.1, ...), kind=kOutput, calls=%fused_computation.324 | convolution fusion | flops 274432000 | bytes 23617540 | tf_op jit(solution)/shard_map/dot_general | solution.py:15
  827.1 40.6 %all-reduce = (f32[2,128]{1,0:T(2,128)}, f32[2,128]{1,0:T(2,128)}) all-reduce(f32[2,128]{1,0:T(2,128)S(1)} %pad_maximum_fusion.4, f32[2,128]{1,0:T(2,128)S(1)} %pad_maximum_fusion.5), channel_id=1, replica_groups=mesh['dp'=8,'head'=4] {'dp','head'}, use_global_device_ids=true, to_apply=%region_48.49 | all-reduce | flops 512 | bytes 4096 | tf_op jit(solution)/shard_map/psum | solution.py:353
  873.3 38.2 %all-reduce.1 = (f32[2,64]{1,0:T(2,128)}, f32[2,32,128]{2,1,0:T(8,128)}, f32[2,128]{1,0:T(2,128)}, f32[2,128]{1,0:T(2,128)}, f32[2,128]{1,0:T(2,128)}, /*index=5*/f32[2,128]{1,0:T(2,128)}, f32[2,128]{1,0:T(2,128)}) all-reduce(f32[2,64]{1,0:T(2,128)S(1)} %pad_maximum_fusion.6, ...), channel_id=1, replica_groups=mesh['dp'=8,'head'=4] {'dp'}, use_global_device_ids=true, to_apply=%region_55.56 | all-reduce | flops 9600 | bytes 76800 | tf_op jit(solution)/shard_map/psum | solution.py:338
  915.7 29.5 %all-reduce.15.cloned.1.call-done = (f32[2,128,96]{1,2,0:T(8,128)}, f32[2,128,128]{2,1,0:T(8,128)}, f32[2,128,128]{2,1,0:T(8,128)}) async-done(((f32[2,128,96]{1,2,0:T(8,128)}, f32[2,128,128]{2,1,0:T(8,128)}, f32[2,128,128]{2,1,0:T(8,128)}), (f32[2,128,96]{1,2,0:T(8,128)}, f32[2,128,128]{2,1,0:T(8,128)}, f32[2,128,128]{2,1,0:T(8,128)})) %all-reduce.15.cloned.1.call-update) | async-done | bytes 360464 | tf_op jit(solution)/shard_map/psum | solution.py:338
  (645 shorter events, 482.5 us)
Async XLA Ops:
  7.2 122.8 %all-gather.11.cloned.1.call-start = ((), (), s32[]{:S(2)}) async-start(), calls=%async_computation.6 | async-start | bytes 2580480 | tf_op jit(solution)/shard_map/all_gather | solution.py:140
  63.0 73.1 %all-gather.5.cloned.1.call-start = ((), (), s32[]{:S(2)}) async-start(), calls=%async_computation.1 | async-start | bytes 2580480 | tf_op jit(solution)/shard_map/all_gather | solution.py:140
  87.2 15.4 %copy-start.26 = (bf16[8,4,250,32]{2,3,1,0:T(8,128)(2,1)}, bf16[8,4,250,32]{2,3,1,0:T(8,128)(2,1)S(1)}, u32[]{:S(2)}) copy-start(bf16[8,4,250,32]{2,3,1,0:T(8,128)(2,1)S(1)} %get-tuple-element.1014) | copy-start | bytes 1536004
  87.2 15.4 %copy-start.27 = (bf16[8,4,250,32]{2,3,1,0:T(8,128)(2,1)}, bf16[8,4,250,32]{2,3,1,0:T(8,128)(2,1)S(1)}, u32[]{:S(2)}) copy-start(bf16[8,4,250,32]{2,3,1,0:T(8,128)(2,1)S(1)} %get-tuple-element.1016) | copy-start | bytes 1536004
  90.2 212.5 %all-gather.9.cloned.1.call-start = ((), (), s32[]{:S(2)}) async-start(), calls=%async_computation.3 | async-start | bytes 2580480 | tf_op jit(solution)/shard_map/all_gather | solution.py:140
  127.4 16.8 %copy-start.60 = (f32[128]{0:T(128)}, f32[128]{0:T(128)S(1)}, u32[]{:S(2)}) copy-start(f32[128]{0:T(128)S(1)} %get-tuple-element.568) | copy-start | bytes 1540
  144.1 94.3 %copy-start.23 = (bf16[8000,128]{0,1:T(8,128)(2,1)}, bf16[8000,128]{0,1:T(8,128)(2,1)S(1)}, u32[]{:S(2)}) copy-start(bf16[8000,128]{0,1:T(8,128)(2,1)S(1)} %add_convert_fusion.1) | copy-start | bytes 6144004
  235.7 37.8 %copy-start.55 = (f32[8,4,250]{2,1,0:T(4,128)}, f32[8,4,250]{2,1,0:T(4,128)S(1)}, u32[]{:S(2)}) copy-start(f32[8,4,250]{2,1,0:T(4,128)S(1)} %get-tuple-element.895) | copy-start | bytes 96004
  238.4 80.3 %all-gather.7.cloned.1.call-start = ((), (), s32[]{:S(2)}) async-start(), calls=%async_computation.2 | async-start | bytes 2580480 | tf_op jit(solution)/shard_map/all_gather | solution.py:140
  291.8 11.0 %copy-start.28 = (bf16[8,4,250,32]{2,3,1,0:T(8,128)(2,1)}, bf16[8,4,250,32]{2,3,1,0:T(8,128)(2,1)S(1)}, u32[]{:S(2)}) copy-start(bf16[8,4,250,32]{2,3,1,0:T(8,128)(2,1)S(1)} %get-tuple-element.1018) | copy-start | bytes 1536004
  291.8 11.0 %copy-start.29 = (bf16[8,4,250,32]{2,3,1,0:T(8,128)(2,1)}, bf16[8,4,250,32]{2,3,1,0:T(8,128)(2,1)S(1)}, u32[]{:S(2)}) copy-start(bf16[8,4,250,32]{2,3,1,0:T(8,128)(2,1)S(1)} %get-tuple-element.1020) | copy-start | bytes 1536004
  293.3 182.3 %all-reduce.9.cloned.1.call-start = ((), (), s32[]{:S(2)}) async-start(), calls=%async_computation.4 | async-start | bytes 4128768 | tf_op jit(solution)/shard_map/psum | solution.py:277
  306.8 16.0 %copy-start.36 = (f32[8000]{0:T(1024)}, f32[8000]{0:T(1024)S(1)}, u32[]{:S(2)}) copy-start(f32[8000]{0:T(1024)S(1)} %broadcast_multiply_fusion.9) | copy-start | bytes 96004
  309.2 13.6 %copy-start.44 = (f32[8000]{0:T(1024)}, f32[8000]{0:T(1024)S(1)}, u32[]{:S(2)}) copy-start(f32[8000]{0:T(1024)S(1)} %add_rsqrt_fusion.1) | copy-start | bytes 96004
  326.6 43.0 %copy-start.24 = (bf16[8000,128]{0,1:T(8,128)(2,1)}, bf16[8000,128]{0,1:T(8,128)(2,1)S(1)}, u32[]{:S(2)}) copy-start(bf16[8000,128]{0,1:T(8,128)(2,1)S(1)} %add_convert_fusion.3) | copy-start | bytes 6144004
  369.6 33.5 %copy-start.30 = (bf16[8000,128]{1,0:T(8,128)(2,1)S(1)}, bf16[8000,128]{1,0:T(8,128)(2,1)}, u32[]{:S(2)}) copy-start(bf16[8000,128]{1,0:T(8,128)(2,1)} %convert_element_type.208) | copy-start | bytes 6144004
  424.6 204.5 %all-reduce.11.cloned.1.call-start = ((), (), s32[]{:S(2)}) async-start(), calls=%async_computation.5 | async-start | bytes 4128768 | tf_op jit(solution)/shard_map/psum | solution.py:319
  543.3 12.6 %copy-start.53 = (bf16[2,128,96]{1,2,0:T(8,128)(2,1)S(1)}, bf16[2,128,96]{1,2,0:T(8,128)(2,1)}, u32[]{:S(2)}) copy-start(bf16[2,128,96]{1,2,0:T(8,128)(2,1)} %param.34) | copy-start | bytes 147460
  578.0 124.3 %all-reduce.13.cloned.1.call-start = ((), (), s32[]{:S(2)}) async-start(), calls=%async_computation.7 | async-start | bytes 4128768 | tf_op jit(solution)/shard_map/psum | solution.py:277
  651.2 260.3 %reduce-scatter.4.cloned.1.call-start = ((), (), s32[]{:S(2)}) async-start(), calls=%async_computation.8 | async-start | bytes 2580480
  651.5 11.2 %copy-start.25 = (bf16[8,4,250,32]{2,3,1,0:T(8,128)(2,1)S(1)}, bf16[8,4,250,32]{2,3,1,0:T(8,128)(2,1)}, u32[]{:S(2)}) copy-start(bf16[8,4,250,32]{2,3,1,0:T(8,128)(2,1)} %get-tuple-element.237) | copy-start | bytes 1536004
  662.7 39.6 %copy-start.13 = (bf16[8000,128]{0,1:T(8,128)(2,1)S(1)}, bf16[8000,128]{0,1:T(8,128)(2,1)}, u32[]{:S(2)}) copy-start(bf16[8000,128]{0,1:T(8,128)(2,1)} %all-reduce.11.cloned.1.call-done) | copy-start | bytes 6144004
  801.9 143.4 %all-reduce.15.cloned.1.call-start = ((), (), s32[]{:S(2)}) async-start(), calls=%async_computation.9 | async-start | bytes 720896 | tf_op jit(solution)/shard_map/psum | solution.py:338
  816.7 52.7 %copy-start.65 = (f32[128]{0:T(128)S(1)}, f32[128]{0:T(128)}, u32[]{:S(2)}) copy-start(f32[128]{0:T(128)} %get-tuple-element.482) | copy-start | bytes 1540
  (63 other events, 329.3 us)
Sparse Core Ops, SparseCore 0:
  63.2 25.0 all-gather.10
  90.3 25.0 all-gather.4
  238.5 25.1 all-gather.8
  293.4 25.1 all-gather.6
  424.7 50.8 all-reduce.8
  578.1 50.9 all-reduce.10
  651.3 50.8 all-reduce.12
  802.0 31.2 reduce-scatter.3
  873.4 71.8 all-reduce.14
where the time goes:
time: 973 us; the launch traced here: 957 us
  matrix products  392 us (40%)
  local copies, waits for them, and re-layouts  214 us (22%)
  waiting for transfers between devices  153 us (16%)
  other arithmetic  94.7 us (10%)
  blocking collectives  84.5 us (9%)
  between operations  16.3 us (2%)
    dot_general x2, matrix products, run_layer(): jnp.dot(act, down_w, preferred_element_type=jnp.float32)  95.8 us
    psum x2, waiting for transfers between devices, shards(): lax.psum(partial_back.astype(jnp.bfloat16), 'head').astype(jnp.float32)  73.3 us
    dot_general x2, matrix products, run_layer(): pre = jnp.dot(norm_two_low, up_w, preferred_element_type=jnp.float32) + up_b  68.6 us
    dot_general x32, matrix products, head_forward(): jnp.einsum('gqk,gkd->gqd', probs_low, value_rows, preferred_element_type=...  42.8 us
    psum x1, waiting for transfers between devices, shards(): lax.psum(head_term.astype(jnp.bfloat16), 'head').astype(jnp.float32)  40.6 us
    psum x1, blocking collectives, shards(): norm_sums = lax.psum((stacked[0], stacked[1]), ('dp', 'head'))  40.6 us
    psum x1, blocking collectives, shards(): lax.psum((stacked[2], stacked[3], stacked[4], stacked[5], stacked[6], sta...  38.2 us
    dot_general x8, matrix products, contract_rows(): lax.dot_general(left_arr, right_arr, (((0,), (0,)), ((), ())), preferred_...  34.4 us
  transfers between devices with their start and end apart: 9, of which 5 were waited for; matrix products, arithmetic and copies ran while one was open for 22% of the time, Pallas kernels for 0%

commit v1 on v0

v1 whole, which is shorter than its diff:
```python
import functools
import math

import jax
import jax.numpy as jnp
from jax import lax
from jax.experimental import pallas as pl
from jax.experimental.pallas import tpu as pltpu
from jax.sharding import PartitionSpec as P

norm_eps = 1e-05
lane = 128
ones_rows = 16
group_size = 8
log2_e = 1.4426950408889634
far_below = -1e30
bf16 = jnp.bfloat16
f32 = jnp.float32


def nn(left, right):
    return lax.dot_general(left, right, (((1,), (0,)), ((), ())), preferred_element_type=f32)


def nt(left, right):
    return lax.dot_general(left, right, (((1,), (1,)), ((), ())), preferred_element_type=f32)


def nt_split(left, right):
    high = right.astype(bf16)
    return nt(left, high) + nt(left, (right - high.astype(f32)).astype(bf16))


def wide(column, width):
    return jnp.concatenate([column] * (width // lane), axis=1)


def gelu_parts(pre):
    cdf = 0.5 * lax.erf(pre * math.sqrt(0.5)) + 0.5
    bell = jnp.exp2((pre * pre) * (-0.5 * log2_e) + math.log2(1.0 / math.sqrt(2.0 * math.pi)))
    return pre * cdf, cdf + pre * bell


def eye(size):
    rows = lax.broadcasted_iota(jnp.int32, (size, size), 0)
    cols = lax.broadcasted_iota(jnp.int32, (size, size), 1)
    return (rows == cols).astype(f32).astype(bf16)


def side_by_side(works, between={}):
    works = [work for work in works if work is not None]
    turn = 0
    while works:
        if turn in between:
            between[turn]()
        works = [work for work in works if next(work, work) is None]
        turn += 1


def fold(block, act):
    rows = [block[i : i + 8] for i in range(0, block.shape[0], 8)]
    return functools.reduce(act, rows)


def spread_rows(block, h, heads):
    size, toks = block.shape
    parts = []
    if h:
        parts.append(jnp.zeros((h * size, toks), block.dtype))
    parts.append(block)
    if h < heads - 1:
        parts.append(jnp.zeros(((heads - 1 - h) * size, toks), block.dtype))
    return jnp.concatenate(parts, axis=0)


class Sizes:
    def __init__(self, slots, win, width, layers, units, heads, groups):
        self.slots, self.win, self.width = slots, win, width
        self.layers, self.units, self.heads, self.groups = layers, units, heads, groups
        self.hd = width // heads
        self.share = units // heads
        self.toks = -(-win // lane) * lane
        self.own = slots // heads
        self.block = 16 if self.own < 16 else self.own
        self.upper_rows = 3 * self.hd + self.hd + width + self.share
        self.first_rows = self.hd + width + self.share
        step = 16 * groups
        round_up = lambda rows: -(-rows // step) * step
        self.early = [
            (self.first_rows, (), round_up(self.first_rows))
            if l == 0
            else (self.upper_rows, (self.first_rows,), round_up(self.upper_rows))
            for l in range(layers)
        ]
        self.late_vec = 3 * self.hd
        self.vec = 16 * -(-8 * layers // 16)
        self.late_used = self.late_vec + self.vec
        self.late = round_up(self.late_used)

    def key(self):
        return (self.slots, self.win, self.width, self.layers, self.units, self.heads, self.groups)


class Reduction:
    def __init__(self, sizes, rows, used, cuts, done, refs):
        self.sizes, self.rows, self.used = sizes, rows, used
        self.chunk = rows // sizes.groups
        (
            self.out_buf,
            self.head_in,
            self.mid,
            self.dp_in,
            self.total,
            self.head_send,
            self.head_recv,
            self.dp_send,
            self.dp_recv,
            self.all_send,
            self.all_recv,
            self.own_sem,
        ) = refs
        self.done = done
        self.cuts = [0] + list(cuts) + [used]
        self.me = lax.axis_index("head")
        self.group = lax.axis_index("dp")

    @staticmethod
    def scratch(sizes, rows, used, width, parts):
        chunk = rows // sizes.groups
        vm = pltpu.VMEM
        dma = pltpu.SemaphoreType.DMA
        return [
            vm((sizes.heads, used, width), bf16),
            vm((sizes.heads - 1, used, width), bf16),
            vm((rows, width), bf16),
            vm((sizes.groups - 1, chunk, width), bf16),
            vm((chunk, width), bf16),
            dma((parts, sizes.heads - 1)),
            dma((parts, sizes.heads - 1)),
            dma((sizes.groups - 1,)),
            dma((sizes.groups - 1,)),
            dma((sizes.groups - 1,)),
            dma((sizes.groups - 1,)),
            dma((1,)),
        ]

    def head_copy(self, k, i):
        peer = lax.rem(self.me + k, self.sizes.heads)
        span = pl.ds(self.cuts[i], self.cuts[i + 1] - self.cuts[i])
        return pltpu.make_async_remote_copy(
            src_ref=self.out_buf.at[peer, span],
            dst_ref=self.head_in.at[k - 1, span],
            send_sem=self.head_send.at[i, k - 1],
            recv_sem=self.head_recv.at[i, k - 1],
            device_id={"head": peer},
            device_id_type=pl.DeviceIdType.MESH,
        )

    def part(self, index):
        return pl.ds(pl.multiple_of(index * self.chunk, 16), self.chunk)

    def dp_copy(self, k):
        peer = lax.rem(self.group + k, self.sizes.groups)
        return pltpu.make_async_remote_copy(
            src_ref=self.mid.at[self.part(peer)],
            dst_ref=self.dp_in.at[k - 1],
            send_sem=self.dp_send.at[k - 1],
            recv_sem=self.dp_recv.at[k - 1],
            device_id={"dp": peer},
            device_id_type=pl.DeviceIdType.MESH,
        )

    def all_copy(self, k):
        peer = lax.rem(self.group + k, self.sizes.groups)
        return pltpu.make_async_remote_copy(
            src_ref=self.total,
            dst_ref=self.done.at[self.part(self.group)],
            send_sem=self.all_send.at[k - 1],
            recv_sem=self.all_recv.at[k - 1],
            device_id={"dp": peer},
            device_id_type=pl.DeviceIdType.MESH,
        )

    def start_heads(self, i):
        for k in range(1, self.sizes.heads):
            self.head_copy(k, i).start()

    def start_groups(self):
        for i in range(len(self.cuts) - 1):
            for k in range(1, self.sizes.heads):
                self.head_copy(k, i).wait()
        total = self.out_buf[self.me].astype(f32)
        for k in range(1, self.sizes.heads):
            total += self.head_in[k - 1].astype(f32)
        self.mid[: self.used] = total.astype(bf16)
        each_peer(self.sizes.groups, lambda k: self.dp_copy(k).start())

    def start_gather(self):
        each_peer(self.sizes.groups, lambda k: self.dp_copy(k).wait())
        own = self.part(self.group)
        total = self.mid[own].astype(f32)
        for k in range(1, self.sizes.groups):
            total += self.dp_in[k - 1].astype(f32)
        self.total[...] = total.astype(bf16)
        self.own_copy().start()
        each_peer(self.sizes.groups, lambda k: self.all_copy(k).start())

    def own_copy(self):
        return pltpu.make_async_copy(
            self.total, self.done.at[self.part(self.group)], self.own_sem.at[0]
        )

    def finish(self):
        self.own_copy().wait()
        each_peer(self.sizes.groups, lambda k: self.all_copy(k).wait())


def each_peer(count, act):
    def step(k, carry):
        act(k)
        return carry

    if count <= 8:
        for k in range(1, count):
            act(k)
    else:
        lax.fori_loop(1, count, step, 0)


def body(sizes, *refs):
    inputs = 18
    early_refs = refs[inputs : inputs + sizes.layers]
    exchange(sizes, early_refs, *refs[:inputs], *refs[inputs + sizes.layers :])


def exchange(
    sizes,
    early_refs,
    count_ref,
    sample_ref,
    x_ref,
    cot_ref,
    qkv_shard_ref,
    qv_ref,
    out_w_ref,
    up_w_ref,
    down_w_ref,
    g1_ref,
    b1_ref,
    bo_ref,
    g2_ref,
    b2_ref,
    bd_ref,
    bu_ref,
    lo_ref,
    ig_ref,
    late_ref,
    stream,
    xh1,
    rs1,
    n1e,
    qkv,
    v_tok,
    probs,
    inv,
    att,
    xh2,
    rs2,
    n2e,
    act,
    slope,
    qkv_t_ref,
    qkv_n,
    out_t,
    up_t,
    down_t,
    cols,
    mask,
    g_qkv,
    g_out,
    g_up,
    g_down,
    g_vec,
    k_tok,
    g_scr,
    gl_kept,
    gp_kept,
    gm_kept,
    gqkv_kept,
    vec_rows,
    lo_stage,
    ig_stage,
    qv_own,
    qv_all,
    shard_send,
    shard_recv,
    qv_send,
    qv_recv,
    lo_send,
    lo_recv,
    ig_send,
    ig_recv,
    own_sem,
    x_in,
    x_rows,
    cot_t,
    in_sem,
    *reduction_refs,
):
    layers, heads, width, units = sizes.layers, sizes.heads, sizes.width, sizes.units
    win, toks, own, hd, share = sizes.win, sizes.toks, sizes.own, sizes.hd, sizes.share
    scale = 1.0 / math.sqrt(hd)
    half = toks // 2
    abreast = math.gcd(own, group_size)
    me = lax.axis_index("head")
    group = lax.axis_index("dp")
    earlies = [
        Reduction(sizes, rows, used, cuts, early_refs[l], reduction_refs[12 * l : 12 * (l + 1)])
        for l, (used, cuts, rows) in enumerate(sizes.early)
    ]
    late = Reduction(sizes, sizes.late, sizes.late_used, (), late_ref, reduction_refs[12 * layers :])

    def head_peer(k):
        return lax.rem(me + k, heads)

    first = me * own
    fetch_from = pl.multiple_of(first // sizes.block * sizes.block, 16)
    fetches = [
        pltpu.make_async_copy(src.at[:, pl.ds(fetch_from, sizes.block)], dst, in_sem.at[i])
        for i, (src, dst) in enumerate(((x_ref, x_in), (cot_ref, x_in)))
    ]
    fetches[0].start()
    barrier = pltpu.get_barrier_semaphore()
    for k in range(1, heads):
        pl.semaphore_signal(
            barrier, inc=1, device_id={"head": head_peer(k)}, device_id_type=pl.DeviceIdType.MESH
        )

    def greet(k):
        pl.semaphore_signal(
            barrier,
            inc=1,
            device_id={"dp": lax.rem(group + k, sizes.groups)},
            device_id_type=pl.DeviceIdType.MESH,
        )

    each_peer(sizes.groups, greet)

    c_g1, c_b1, c_qkv, c_bo = 0, width, 2 * width, 5 * width
    c_g2, c_b2, c_bd, c_up = 6 * width, 7 * width, 8 * width, 9 * width

    identity = eye(width)
    identity_tok = eye(toks)

    def row_to_column(row):
        return jnp.transpose(jnp.broadcast_to(row, (lane, lane)))

    qv_own[...] = jnp.zeros_like(qv_own)
    for l in range(layers):
        qv_own[l : l + 1, :hd] = qv_ref[l : l + 1, :hd]
        qv_own[l : l + 1, 2 * hd : 3 * hd] = qv_ref[l : l + 1, hd : 2 * hd]
    mine = pl.ds(pl.multiple_of(me * 3 * hd, 16), 3 * hd)
    own_shard = pltpu.make_async_copy(qkv_shard_ref, qkv_t_ref.at[:, mine], own_sem.at[0])
    own_qv = pltpu.make_async_copy(qv_own, qv_all.at[me], own_sem.at[1])

    def shard_copy(k):
        return pltpu.make_async_remote_copy(
            src_ref=qkv_shard_ref,
            dst_ref=qkv_t_ref.at[:, mine],
            send_sem=shard_send.at[k - 1],
            recv_sem=shard_recv.at[k - 1],
            device_id={"head": head_peer(k)},
            device_id_type=pl.DeviceIdType.MESH,
        )

    def qv_copy(k):
        return pltpu.make_async_remote_copy(
            src_ref=qv_own,
            dst_ref=qv_all.at[me],
            send_sem=qv_send.at[k - 1],
            recv_sem=qv_recv.at[k - 1],
            device_id={"head": head_peer(k)},
            device_id_type=pl.DeviceIdType.MESH,
        )

    pl.semaphore_wait(barrier, heads - 1 + sizes.groups - 1)
    own_shard.start()
    own_qv.start()
    for k in range(1, heads):
        qv_copy(k).start()
        shard_copy(k).start()

    def sort_rows(src, dst):
        step = 10 if win % 10 == 0 else 1
        for t in range(0, win, step):
            block = src[t : t + step].astype(f32)
            rows = block[:, :own]
            for i in range(1, sizes.block // own):
                here = first - fetch_from == i * own
                rows = jnp.where(here, block[:, i * own : (i + 1) * own], rows)
            dst[t * own : (t + step) * own] = rows.reshape(step * own, width)
        dst[win * own :] = jnp.zeros(((toks - win) * own, width), f32)

    def turned(src, w):
        return nt(identity, src[pl.ds(w, toks, stride=own), :].astype(bf16))

    def put_column(l, start, ref):
        cols[l, start : start + width] = row_to_column(ref[l : l + 1, :])

    for l in range(layers):
        out_t[l] = nt(identity, out_w_ref[l]).astype(bf16)
        for part in range(units // width):
            span = slice(part * width, (part + 1) * width)
            up_t[l, span, :] = jnp.transpose(up_w_ref[l, :, span].astype(f32)).astype(bf16)
            cols[l, c_up + part * width : c_up + (part + 1) * width] = row_to_column(
                bu_ref[l : l + 1, span]
            )
        down_t[l] = nt(identity, down_w_ref[l]).astype(bf16)
        for start, ref in (
            (c_bo, bo_ref),
            (c_g2, g2_ref),
            (c_b2, b2_ref),
            (c_bd, bd_ref),
        ):
            put_column(l, start, ref)
        put_column(l, c_g1, g1_ref)
        put_column(l, c_b1, b1_ref)
    key_pos = lax.broadcasted_iota(jnp.int32, (half, half), 0)
    query_pos = lax.broadcasted_iota(jnp.int32, (half, half), 1)
    mask[...] = jnp.where(key_pos <= query_pos, 0.0, far_below)
    g_vec[...] = jnp.zeros_like(g_vec)
    vec_rows[...] = jnp.zeros_like(vec_rows)
    for packet in earlies + [late]:
        if packet.rows > packet.used:
            packet.mid[packet.used :] = jnp.zeros((packet.rows - packet.used, width), bf16)

    for w in range(own):
        for l in range(layers):
            n1e[l, w, width:, :] = jnp.ones((ones_rows, toks), bf16)
            n2e[l, w, width:, :] = jnp.ones((ones_rows, toks), bf16)
            att[l, w, width:, :] = jnp.ones((ones_rows, toks), bf16)
            act[l, w, units:, :] = jnp.ones((ones_rows, toks), bf16)
        for h in range(heads):
            g_scr[w, h, half:, :half] = jnp.zeros((half, half), bf16)
            for l in range(layers):
                probs[l, w, h, half:, :half] = jnp.zeros((half, half), bf16)

    fetches[0].wait()
    sort_rows(x_in, x_rows)
    fetches[1].start()
    for w in range(own):
        stream[w] = turned(x_rows, w)

    fetches[1].wait()
    sort_rows(x_in, x_rows)
    for w in range(own):
        cot_t[w] = turned(x_rows, w).astype(bf16)

    def col(l, start, count):
        return wide(cols[l, start : start + count, :], toks)

    step = hd


    def spans(start, count):
        return [slice(r, r + step) for r in range(start, start + count, step)]

    def norm(w, l, gain, shift, unit_ref, spread_ref, low_ref):
        total = sum(fold(stream[w, r], jnp.add) for r in spans(0, width))
        mean = jnp.sum(total, axis=0, keepdims=True) * (1.0 / width)
        square = 0.0
        for r in spans(0, width):
            center = stream[w, r] - mean
            square += fold(center * center, jnp.add)
        spread = lax.rsqrt(jnp.sum(square, axis=0, keepdims=True) * (1.0 / width) + norm_eps)
        spread_ref[l, w] = spread
        for r in spans(0, width):
            unit = (stream[w, r] - mean) * spread
            unit_ref[l, w, r] = unit
            low_ref[l, w, r] = (
                unit * col(l, gain + r.start, step) + col(l, shift + r.start, step)
            ).astype(bf16)

    for w in range(own):
        norm(w, 0, c_g1, c_b1, xh1, rs1, n1e)
    own_shard.wait()
    own_qv.wait()
    for k in range(1, heads):
        qv_copy(k).wait()
        shard_copy(k).wait()
    for l in range(layers):
        qkv_n[l] = nt(identity, qkv_t_ref[l]).astype(bf16)
        for h in range(heads):
            cols[l, c_qkv + 3 * hd * h : c_qkv + 3 * hd * (h + 1)] = row_to_column(
                qv_all[h, l : l + 1, :]
            )[: 3 * hd]
    def forward(l, w):
        if l:
            norm(w, l, c_g1, c_b1, xh1, rs1, n1e)
            yield
        made = nn(qkv_t_ref[l], n1e[l, w, :width])
        for i, r in enumerate(spans(0, 3 * width)):
            piece = made[r] + col(l, c_qkv + r.start, step)
            qkv[l, w, r] = (piece if i % 3 else piece * (scale * log2_e)).astype(bf16)
        yield
        rows_of = lambda h, which: slice((3 * h + which) * hd, (3 * h + which + 1) * hd)
        kv_all = jnp.concatenate(
            [qkv[l, w, rows_of(h, which)] for which in (1, 2) for h in range(heads)], axis=0
        )
        made = nt(identity_tok, kv_all)
        for r in spans(0, toks):
            k_tok[w, r] = made[r, :width].astype(bf16)
            v_tok[l, w, r] = made[r, width:].astype(bf16)
        for h in range(heads):
            yield
            s = nn(k_tok[w], spread_rows(qkv[l, w, rows_of(h, 0)], h, heads))
            top0 = top1 = None
            for r in spans(0, half):
                far = slice(r.start + half, r.stop + half)
                new0 = fold(s[r, :half] + mask[r], jnp.maximum)
                new1 = jnp.maximum(
                    fold(s[r, half:], jnp.maximum), fold(s[far, half:] + mask[r], jnp.maximum)
                )
                top0 = new0 if top0 is None else jnp.maximum(top0, new0)
                top1 = new1 if top1 is None else jnp.maximum(top1, new1)
            top0 = jnp.max(top0, axis=0, keepdims=True)
            top1 = jnp.max(top1, axis=0, keepdims=True)
            for r in spans(0, half):
                far = slice(r.start + half, r.stop + half)
                probs[l, w, h, r, :half] = jnp.exp2(s[r, :half] + mask[r] - top0).astype(bf16)
                probs[l, w, h, r, half:] = jnp.exp2(s[r, half:] - top1).astype(bf16)
                probs[l, w, h, far, half:] = jnp.exp2(s[far, half:] + mask[r] - top1).astype(bf16)
            yield
            v_ext = jnp.concatenate(
                [qkv[l, w, rows_of(h, 2)], jnp.ones((ones_rows, toks), bf16)], axis=0
            )
            o = nn(v_ext, probs[l, w, h])
            inverse = 1.0 / o[hd : hd + 1]
            inv[l, w, h] = inverse
            att[l, w, hd * h : hd * (h + 1)] = (o[:hd] * inverse).astype(bf16)
        yield
        made = nn(out_t[l], att[l, w, :width])
        for r in spans(0, width):
            stream[w, r] = stream[w, r] + made[r] + col(l, c_bo + r.start, step)
        norm(w, l, c_g2, c_b2, xh2, rs2, n2e)
        yield
        made = nn(up_t[l], n2e[l, w, :width])
        for r in spans(0, units):
            a, sl = gelu_parts(made[r] + col(l, c_up + r.start, step))
            act[l, w, r] = a.astype(bf16)
            slope[l, w, r] = sl.astype(bf16)
        yield
        made = nn(down_t[l], act[l, w, :units])
        for r in spans(0, width):
            value = stream[w, r] + made[r] + col(l, c_bd + r.start, step)
            if l < layers - 1:
                stream[w, r] = value
            else:
                lo_stage[r.start // hd, w] = value.astype(bf16)

    def norm_sums(l, w, grad, gain, unit_ref, which):
        plain = tilted = 0.0
        for r in spans(0, width):
            by_unit = grad[r] * unit_ref[l, w, r]
            at = slice(which * width + r.start, which * width + r.stop)
            g_vec[l, at] += by_unit
            at = slice((which + 1) * width + r.start, (which + 1) * width + r.stop)
            g_vec[l, at] += grad[r]
            column = col(l, gain + r.start, step)
            plain += fold(grad[r] * column, jnp.add)
            tilted += fold(by_unit * column, jnp.add)
        return (
            jnp.sum(plain, axis=0, keepdims=True) * (1.0 / width),
            jnp.sum(tilted, axis=0, keepdims=True) * (1.0 / width),
        )

    def norm_back(l, w, grad, gain, unit_ref, spread_ref, means, emit):
        spread = spread_ref[l, w]
        for r in spans(0, width):
            s = grad[r] * col(l, gain + r.start, step)
            emit(r, stream[w, r] + spread * (s - means[0] - unit_ref[l, w, r] * means[1]))

    def backward_units(l, w):
        if l == layers - 1:
            slot = me * own + w
            weight = jnp.where(slot < count_ref[0], sample_ref[slot], 0.0)
        for r in spans(0, width):
            if l == layers - 1:
                stream[w, r] = cot_t[w, r].astype(f32) * weight
            gl_kept[w, r] = stream[w, r].astype(bf16)
        yield
        made = nn(down_w_ref[l], gl_kept[w])
        for r in spans(0, units):
            gp_kept[w, r] = made[r].astype(bf16) * slope[l, w, r]
        yield
        gn = nn(up_w_ref[l], gp_kept[w])
        yield
        means = norm_sums(l, w, gn, c_g2, xh2, 2)

        def emit(r, value):
            stream[w, r] = value
            gm_kept[w, r] = value.astype(bf16)

        norm_back(l, w, gn, c_g2, xh2, rs2, means, emit)

    def backward_attention(l, w, after):
        ga = nn(out_w_ref[l], gm_kept[w])
        shares, dots = [], []
        for h in range(heads):
            rows = slice(h * hd, (h + 1) * hd)
            gs = (ga[rows] * inv[l, w, h]).astype(bf16)
            shares.append(gs)
            dots.append(
                jnp.sum(gs.astype(f32) * att[l, w, rows, :].astype(f32), axis=0, keepdims=True)
            )
        yield
        for h in range(heads):
            base = 3 * h * hd
            yield
            gs, dot = shares[h], dots[h]
            made = nn(v_tok[l, w], spread_rows(gs, h, heads))
            gqkv_kept[w, base + 2 * hd : base + 3 * hd] = nt(gs, probs[l, w, h]).astype(bf16)
            d0, d1 = dot[:, :half], dot[:, half:]
            for r in spans(0, half):
                far = slice(r.start + half, r.stop + half)
                g_scr[w, h, r, :half] = probs[l, w, h, r, :half] * (made[r, :half] - d0).astype(bf16)
                g_scr[w, h, r, half:] = probs[l, w, h, r, half:] * (made[r, half:] - d1).astype(bf16)
                g_scr[w, h, far, half:] = probs[l, w, h, far, half:] * (
                    made[far, half:] - d1
                ).astype(bf16)
            yield
            q = qkv[l, w, base : base + hd, :]
            k = qkv[l, w, base + hd : base + 2 * hd, :]
            g = g_scr[w, h]
            gq = (nn(k, g) * scale).astype(bf16)
            gk = (nt(q, g) * (1.0 / log2_e)).astype(bf16)
            gqkv_kept[w, base : base + hd] = gq
            gqkv_kept[w, base + hd : base + 2 * hd] = gk
        yield
        gn = nn(qkv_n[l], gqkv_kept[w])
        yield
        means = norm_sums(l, w, gn, c_g1, xh1, 0)
        after(w, gn, means)

    def lanes(ref, ws):
        return jnp.concatenate([ref[w] for w in ws], axis=1)

    def unit_sums(l, ws):
        def add(ref, value):
            ref[l] = value if ws[0] == 0 else ref[l] + value

        add(g_down, nt(lanes(act.at[l], ws), lanes(gl_kept, ws)))
        add(g_up, nt(lanes(n2e.at[l], ws), lanes(gp_kept, ws)))
        add(g_out, nt(lanes(att.at[l], ws), lanes(gm_kept, ws)))

    def qkv_sums(l, ws):
        value = nt(lanes(gqkv_kept, ws), lanes(n1e.at[l], ws))
        g_qkv[l] = value if ws[0] == 0 else g_qkv[l] + value

    def run(step, first, last, width=1):
        def inner(i, carry):
            side_by_side([step(first + i * width + u) for u in range(width)])
            return carry

        if last - first == width:
            inner(0, 0)
        else:
            lax.fori_loop(0, (last - first) // width, inner, 0)

    last = math.gcd(own, 4)
    cut = own - last

    def lo_copy(k):
        peer = head_peer(k)
        return pltpu.make_async_remote_copy(
            src_ref=lo_stage.at[peer],
            dst_ref=lo_ref.at[pl.ds(me * own, own)],
            send_sem=lo_send.at[k - 1],
            recv_sem=lo_recv.at[k - 1],
            device_id={"head": peer},
            device_id_type=pl.DeviceIdType.MESH,
        )

    def ig_copy(k, i):
        peer = head_peer(k)
        return pltpu.make_async_remote_copy(
            src_ref=ig_stage.at[peer, pl.ds(i * last, last)],
            dst_ref=ig_ref.at[pl.ds(me * own + i * last, last)],
            send_sem=ig_send.at[k - 1, i],
            recv_sem=ig_recv.at[k - 1, i],
            device_id={"head": peer},
            device_id_type=pl.DeviceIdType.MESH,
        )

    for l in range(layers):
        run(functools.partial(forward, l), 0, own, abreast)

    own_lo = pltpu.make_async_copy(
        lo_stage.at[me], lo_ref.at[pl.ds(me * own, own)], own_sem.at[2]
    )
    own_lo.start()
    for k in range(1, heads):
        lo_copy(k).start()

    def vector_rows(l, norm_index):
        at = slice(2 * norm_index * width, 2 * (norm_index + 1) * width)
        return nt_split(jnp.ones((16, toks), bf16), g_vec[l, at])

    def qkv_bias_rows(l):
        at = lax.broadcasted_iota(jnp.int32, (16, width + ones_rows), 1)
        return nt_split((at == width).astype(f32).astype(bf16), g_qkv[l])

    def pack_units(l):
        buf = earlies[l].out_buf
        for h in range(heads):
            at = 0
            buf[h, at : at + hd] = g_out[l, hd * h : hd * (h + 1), :].astype(bf16)
            at += hd
            buf[h, at : at + width] = g_up[l, :width, share * h : share * (h + 1)].astype(bf16)
            at += width
            buf[h, at : at + share] = g_down[l, share * h : share * (h + 1), :].astype(bf16)

    def pack_qkv(l):
        r = sizes.first_rows
        for h in range(heads):
            earlies[l].out_buf[h, r : r + 3 * hd] = g_qkv[
                l, 3 * hd * h : 3 * hd * (h + 1), :width
            ].astype(bf16)

    def put_row(at, row):
        for h in range(heads):
            vec_rows[h, at : at + 1] = row

    def put_norm(l, norm_index, at):
        sums = vector_rows(l, norm_index)
        put_row(at, sums[:1, :width])
        put_row(at + 1, sums[:1, width:])

    def put_qkv(l):
        biases = qkv_bias_rows(l)
        for h in range(heads):
            for i in range(3):
                at = (3 * h + i) * hd
                vec_rows[h, 8 * l + 7 : 8 * l + 8, i * hd : (i + 1) * hd] = biases[:1, at : at + hd]

    def pack_vectors():
        for l in range(layers):
            v = 8 * l
            if l:
                put_norm(l, 0, v)
                put_qkv(l)
            put_row(v + 2, g_out[l, width : width + 1, :])
            put_norm(l, 1, v + 3)
            put_row(v + 5, g_down[l, units : units + 1, :])
            for h in range(heads):
                vec_rows[h, v + 6 : v + 7] = g_up[
                    l, width : width + 1, share * h : share * (h + 1)
                ]

    def pack_late():
        put_norm(0, 0, 0)
        put_qkv(0)
        for h in range(heads):
            late.out_buf[h, : 3 * hd] = g_qkv[0, 3 * hd * h : 3 * hd * (h + 1), :width].astype(
                bf16
            )
            late.out_buf[h, 3 * hd :] = vec_rows[h].astype(bf16)

    def give(w, gn, means):
        def emit(r, value):
            ig_stage[r.start // hd, w] = value.astype(bf16)

        norm_back(0, w, gn, c_g1, xh1, rs1, means, emit)
    waiting = {}

    def keep(w, gn, means):
        for i in range(toks // lane):
            at = (w * (toks // lane) + i) * width
            x_rows[at : at + width] = gn[:, i * lane : (i + 1) * lane]
        waiting[w] = means

    everyone = list(range(own))
    for l in range(layers - 1, -1, -1):
        run(functools.partial(backward_units, l), 0, own, abreast)
        steps = {}
        if l < layers - 1:
            steps[heads + 2] = earlies[l + 1].start_gather
        if l:

            def settle(w, gn, means, l=l):
                def emit(r, value):
                    stream[w, r] = value

                norm_back(l, w, gn, c_g1, xh1, rs1, means, emit)

            def unit_step(l=l):
                unit_sums(l, everyone)
                pack_units(l)
                earlies[l].start_heads(0)

            steps[heads] = unit_step
        else:
            settle = keep
            unit_sums(l, everyone)
            pack_units(l)
            earlies[l].start_heads(0)
            steps[2] = pack_vectors
            steps[2 * heads] = earlies[l].start_groups
        if l < layers - 1:
            earlies[l + 1].start_groups()
        side_by_side([backward_attention(l, w, after=settle) for w in everyone], steps)
        if l:
            qkv_sums(l, everyone)
            pack_qkv(l)
            earlies[l].start_heads(1)

    qkv_sums(0, everyone)
    pack_late()
    late.start_heads(0)
    earlies[0].start_gather()
    batches = own // last

    def give_batch(i):
        for w in everyone[i * last : (i + 1) * last]:
            at = w * (toks // lane) * width
            halves = [x_rows[at + i * width : at + (i + 1) * width] for i in range(toks // lane)]
            give(w, jnp.concatenate(halves, axis=1), waiting[w])

    def send_batch(i):
        for k in range(1, heads):
            ig_copy(k, i).start()

    for i in range(batches - 1):
        give_batch(i)
        send_batch(i)
    give_batch(batches - 1)
    own_ig = pltpu.make_async_copy(
        ig_stage.at[me], ig_ref.at[pl.ds(me * own, own)], own_sem.at[3]
    )
    late.start_groups()
    send_batch(batches - 1)
    own_ig.start()
    own_lo.wait()
    for k in range(1, heads):
        lo_copy(k).wait()
    late.start_gather()
    for packet in earlies:
        packet.finish()
    for i in range(batches):
        for k in range(1, heads):
            ig_copy(k, i).wait()
    own_ig.wait()
    late.finish()


def finish_body(sizes, lo_in, ig_in, *refs):
    packets = refs[: sizes.layers + 1]
    write_outputs(sizes, lo_in, ig_in, packets[:-1], packets[-1], *refs[sizes.layers + 1 :])


def write_outputs(
    sizes,
    lo_in,
    ig_in,
    earlies_in,
    late_in,
    lo_out,
    ig_out,
    ln1_g,
    ln1_s,
    qkv_g,
    qv_g,
    out_g,
    out_b,
    ln2_g,
    ln2_s,
    up_g,
    up_b,
    down_g,
    down_b,
):
    hd, width, share = sizes.hd, sizes.width, sizes.share
    lo_out[...] = lo_in[...][:, :, : sizes.win]
    ig_out[...] = ig_in[...][:, :, : sizes.win].astype(f32)
    for l in range(sizes.layers):
        at = 0
        early_in = earlies_in[l]
        out_g[l] = early_in[at : at + hd].astype(f32)
        at += hd
        up_g[l] = early_in[at : at + width].astype(f32)
        at += width
        down_g[l] = early_in[at : at + share].astype(f32)
        at += share
        if l:
            qkv_g[l] = early_in[at : at + 3 * hd].astype(f32)
            at += 3 * hd
        else:
            qkv_g[l] = late_in[: 3 * hd].astype(f32)
    vec = late_in[3 * hd : 3 * hd + sizes.vec].astype(f32)
    for l in range(sizes.layers):
        v = 8 * l
        row = slice(l, l + 1)
        ln1_g[row] = vec[v : v + 1]
        ln1_s[row] = vec[v + 1 : v + 2]
        out_b[row] = vec[v + 2 : v + 3]
        ln2_g[row] = vec[v + 3 : v + 4]
        ln2_s[row] = vec[v + 4 : v + 5]
        down_b[row] = vec[v + 5 : v + 6]
        up_b[row] = vec[v + 6 : v + 7]
        qv = vec[v + 7 : v + 8]
        qv_g[row, :hd] = qv[:, :hd]
        qv_g[row, hd:] = qv[:, 2 * hd : 3 * hd]


def exchange_pass(sizes, count, sample, x, cot, shard, qv, big, small):
    layers, heads, width, units = sizes.layers, sizes.heads, sizes.width, sizes.units
    own, toks, hd, win = sizes.own, sizes.toks, sizes.hd, sizes.win
    vm = lambda *shape: pltpu.VMEM(shape[:-1], shape[-1])
    dma = pltpu.SemaphoreType.DMA
    whole = pl.BlockSpec(memory_space=pltpu.VMEM)
    scalars = pl.BlockSpec(memory_space=pltpu.SMEM)
    left = pl.BlockSpec(memory_space=pl.ANY)
    return pl.pallas_call(
        functools.partial(body, sizes),
        out_shape=(
            jax.ShapeDtypeStruct((sizes.slots, hd, toks), bf16),
            jax.ShapeDtypeStruct((sizes.slots, hd, toks), bf16),
            *[jax.ShapeDtypeStruct((rows, width), bf16) for _, _, rows in sizes.early],
            jax.ShapeDtypeStruct((sizes.late, width), bf16),
        ),
        in_specs=[scalars, scalars, left, left] + [whole] * 12,
        out_specs=(left,) * (layers + 3),
        scratch_shapes=[
            vm(own, width, toks, f32),
            vm(layers, own, width, toks, f32),
            vm(layers, own, 1, toks, f32),
            vm(layers, own, width + ones_rows, toks, bf16),
            vm(layers, own, 3 * width, toks, bf16),
            vm(layers, own, toks, width, bf16),
            vm(layers, own, heads, toks, toks, bf16),
            vm(layers, own, heads, 1, toks, f32),
            vm(layers, own, width + ones_rows, toks, bf16),
            vm(layers, own, width, toks, f32),
            vm(layers, own, 1, toks, f32),
            vm(layers, own, width + ones_rows, toks, bf16),
            vm(layers, own, units + ones_rows, toks, bf16),
            vm(layers, own, units, toks, bf16),
            vm(layers, 3 * width, width, bf16),
            vm(layers, width, 3 * width, bf16),
            vm(layers, width, width, bf16),
            vm(layers, units, width, bf16),
            vm(layers, width, units, bf16),
            vm(layers, 9 * width + units, lane, f32),
            vm(toks // 2, toks // 2, f32),
            vm(layers, 3 * width, width + ones_rows, f32),
            vm(layers, width + ones_rows, width, f32),
            vm(layers, width + ones_rows, units, f32),
            vm(layers, units + ones_rows, width, f32),
            vm(layers, 4 * width, toks, f32),
            vm(own, toks, width, bf16),
            vm(own, heads, toks, toks, bf16),
            vm(own, width, toks, bf16),
            vm(own, units, toks, bf16),
            vm(own, width, toks, bf16),
            vm(own, 3 * width, toks, bf16),
            vm(heads, sizes.vec, width, f32),
            vm(heads, own, hd, toks, bf16),
            vm(heads, own, hd, toks, bf16),
            vm(8, lane, f32),
            vm(heads, 8, lane, f32),
            dma((heads - 1,)),
            dma((heads - 1,)),
            dma((heads - 1,)),
            dma((heads - 1,)),
            dma((heads - 1,)),
            dma((heads - 1,)),
            dma((heads - 1, own)),
            dma((heads - 1, own)),
            dma((4,)),
            vm(win, sizes.block, width, bf16),
            vm(toks * own, width, f32),
            vm(own, width, toks, bf16),
            dma((2,)),
        ]
        + [
            ref
            for used, cuts, rows in sizes.early
            for ref in Reduction.scratch(sizes, rows, used, width, len(cuts) + 1)
        ]
        + Reduction.scratch(sizes, sizes.late, sizes.late_used, width, 1),
        compiler_params=pltpu.CompilerParams(
            vmem_limit_bytes=63 * 1024 * 1024, collective_id=0, has_side_effects=True
        ),
    )(count, sample, x, cot, shard, qv, *big, *small)


def finish_pass(sizes, lo, ig, *packets):
    layers, width, hd, share = sizes.layers, sizes.width, sizes.hd, sizes.share
    whole = pl.BlockSpec(memory_space=pltpu.VMEM)
    out = lambda *shape: jax.ShapeDtypeStruct(shape, f32)
    row = out(layers, width)
    final = (sizes.slots, hd, sizes.win)
    return pl.pallas_call(
        functools.partial(finish_body, sizes),
        out_shape=(
            jax.ShapeDtypeStruct(final, bf16),
            out(*final),
            row,
            row,
            out(layers, 3 * hd, width),
            out(layers, 2 * hd),
            out(layers, hd, width),
            row,
            row,
            row,
            out(layers, width, share),
            out(layers, share),
            out(layers, share, width),
            row,
        ),
        in_specs=[whole] * (2 + len(packets)),
        out_specs=(whole,) * 14,
        compiler_params=pltpu.CompilerParams(vmem_limit_bytes=60 * 1024 * 1024),
    )(lo, ig, *packets)


def shards(
    layer_input,
    cotangent,
    window_count,
    sample_weight,
    ln1_gain,
    ln1_shift,
    qkv_weight,
    qv_bias,
    out_weight,
    out_bias,
    ln2_gain,
    ln2_shift,
    up_weight,
    up_bias,
    down_weight,
    down_bias,
):
    slots, win, width = layer_input.shape
    layers, _, units = up_weight.shape
    sizes = Sizes(
        slots, win, width, layers, units, lax.axis_size("head"), lax.axis_size("dp")
    )
    lo, ig, *packets = exchange_pass(
        sizes,
        window_count,
        sample_weight,
        jnp.swapaxes(layer_input, 0, 1),
        jnp.swapaxes(cotangent, 0, 1),
        jnp.swapaxes(qkv_weight, 1, 2),
        qv_bias,
        (out_weight, up_weight, down_weight),
        (ln1_gain, ln1_shift, out_bias, ln2_gain, ln2_shift, down_bias, up_bias),
    )
    outs = list(finish_pass(sizes, lo, ig, *packets))
    for index in (0, 1, 4):
        outs[index] = jnp.swapaxes(outs[index], 1, 2)
    return tuple(outs)


def solution(mesh):
    return jax.shard_map(
        shards,
        mesh=mesh,
        in_specs=(
            P("dp", None, None),
            P("dp", None, None),
            P("dp"),
            P("dp"),
            P(),
            P(),
            P(None, None, "head"),
            P(None, "head"),
            P(),
            P(),
            P(),
            P(),
            P(),
            P(),
            P(),
            P(),
        ),
        out_specs=(
            P("dp", None, "head"),
            P("dp", None, "head"),
            P(),
            P(),
            P(None, None, "head"),
            P(None, "head"),
            P(None, "head", None),
            P(),
            P(),
            P(),
            P(None, None, "head"),
            P(None, "head"),
            P(None, "head", None),
            P(),
        ),
        check_vma=False,
    )
```

time: 973 us -> 58.3 us (0.06); the launches traced: 957 us -> 58.1 us
  matrix products: 392 us -> 0 us
  local copies, waits for them, and re-layouts: 214 us -> 0 us
  waiting for transfers between devices: 153 us -> 0 us
  other arithmetic: 94.7 us -> 0 us
  blocking collectives: 84.5 us -> 0 us
  Pallas kernels: 0 us -> 56.6 us
  between operations: 16.3 us -> 1.48 us
    dot_general x154 -> x0, matrix products: 383 us -> none  [the longest x2 95.8 us: run_layer(): jnp.dot(act, down_w, preferred_element_type=jnp.float32)]
    psum x4 -> x0, waiting for transfers between devices: 143 us -> none  [the longest x2 73.3 us: shards(): lax.psum(partial_back.astype(jnp.bfloat16), 'head').astype(jnp.float32)]
    psum x3 -> x0, blocking collectives: 84.5 us -> none  [the longest x1 40.6 us: shards(): norm_sums = lax.psum((stacked[0], stacked[1]), ('dp', 'head'))]
    pallas_call x0 -> x2, Pallas kernels: none -> 56.6 us  [the longest x1 54 us: exchange_pass(): pl.pallas_call(functools.partial(body, sizes), out_shape=(jax.ShapeDtypeS...]
    reshape x14 -> x0, local copies, waits for them, and re-layouts: 54.7 us -> none  [the longest x2 14.4 us: split_heads(): qkv_rows.reshape(slot_count // window_group, window_group, window_len, 3...]
    reduce_sum x32 -> x0, other arithmetic: 49.2 us -> none  [the longest x2 10.4 us: shards(): jnp.sum(grad_norm_two * unit_two, axis=0).astype(jnp.bfloat16)]
    unnamed x169 -> x0, local copies, waits for them, and re-layouts: 29.9 us -> none
    dot_general x4 -> x0, local copies, waits for them, and re-layouts: 22.8 us -> none  [contract_cols(): lax.dot_general(left_arr, right_arr, (((1,), (1,)), ((), ())), preferred_...]
  transfers between devices with their start and end apart: 9 -> 0, of which waited for: 5 -> 0; matrix products, arithmetic and copies ran while one was open for 22% -> 0% of each run, Pallas kernels for 0% -> 0%
where the time goes in v1:
time: 58.3 us; the launch traced here: 58.1 us
  Pallas kernels  56.6 us (97%)
  between operations  1.48 us (3%)
    pallas_call x1, Pallas kernels, exchange_pass(): pl.pallas_call(functools.partial(body, sizes), out_shape=(jax.ShapeDtypeS...  54 us
    pallas_call x1, Pallas kernels, finish_pass(): pl.pallas_call(functools.partial(finish_body, sizes), out_shape=(jax.Shap...  2.63 us

profile of v1, /device:TPU:0, one launch (start us, length us, event | category | flops | bytes accessed | tf_op | source)
XLA Modules:
  0.0 58.1 jit_solution(2830973839351552826)
XLA Ops:
  1.3 54.0 %shard_map.263 = (bf16[32,32,256]{2,1,0:T(8,128)(2,1)}, bf16[32,32,256]{2,1,0:T(8,128)(2,1)}, bf16[384,128]{1,0:T(8,128)(2,1)}, bf16[384,128]{1,0:T(8,128)(2,1)}, bf16[128,128]{1,0:T(8,128)(2,1)}) custom-call(s32[1]{0:T(128)S(6)} %copy.30.refs_0_, f32[32]{0:T(128)} %refs_1_.1, bf16[250,32,128]{2,1,0:T(8,128)(2,1)} %bitcast.6, bf16[250,32,128]{2,1,0:T(8,128)(2,1)} %bitcast.7, ...), custom_call_target="tpu_custom_call" | custom-call | tf_op jit(solution)/shard_map/pallas_call | solution.py:923
  55.3 2.6 %shard_map.264 = (bf16[32,32,250]{2,1,0:T(8,128)(2,1)}, f32[32,32,250]{2,1,0:T(8,128)}, f32[2,128]{1,0:T(2,128)}, f32[2,128]{1,0:T(2,128)}, f32[2,96,128]{2,1,0:...) custom-call(bf16[32,32,256]{2,1,0:T(8,128)(2,1)} %get-tuple-element., ...), custom_call_target="tpu_custom_call" | custom-call | tf_op jit(solution)/shard_map/pallas_call | solution.py:1003

commit v2 on v1

--- a/solution.py
+++ b/solution.py
@@ -451,11 +451,6 @@
     for w in range(own):
         stream[w] = turned(x_rows, w)
 
-    fetches[1].wait()
-    sort_rows(x_in, x_rows)
-    for w in range(own):
-        cot_t[w] = turned(x_rows, w).astype(bf16)
-
     def col(l, start, count):
         return wide(cols[l, start : start + count, :], toks)
 
@@ -494,6 +489,11 @@
             cols[l, c_qkv + 3 * hd * h : c_qkv + 3 * hd * (h + 1)] = row_to_column(
                 qv_all[h, l : l + 1, :]
             )[: 3 * hd]
+    fetches[1].wait()
+    sort_rows(x_in, x_rows)
+    for w in range(own):
+        cot_t[w] = turned(x_rows, w).astype(bf16)
+
     def forward(l, w):
         if l:
             norm(w, l, c_g1, c_b1, xh1, rs1, n1e)
@@ -817,7 +817,6 @@
     qkv_sums(0, everyone)
     pack_late()
     late.start_heads(0)
-    earlies[0].start_gather()
     batches = own // last
 
     def give_batch(i):
@@ -838,6 +837,7 @@
         ig_stage.at[me], ig_ref.at[pl.ds(me * own, own)], own_sem.at[3]
     )
     late.start_groups()
+    earlies[0].start_gather()
     send_batch(batches - 1)
     own_ig.start()
     own_lo.wait()

time: 58.3 us -> 58.1 us (level)
  no operation moved by 1% of the time
where the time goes in v2:
time: 58.1 us; the launch traced here: 57.9 us
  Pallas kernels  56.4 us (97%)
  between operations  1.48 us (3%)
    pallas_call x1, Pallas kernels, exchange_pass(): pl.pallas_call(functools.partial(body, sizes), out_shape=(jax.ShapeDtypeS...  53.8 us
    pallas_call x1, Pallas kernels, finish_pass(): pl.pallas_call(functools.partial(finish_body, sizes), out_shape=(jax.Shap...  2.63 us

profile of v2, /device:TPU:0, one launch (start us, length us, event | category | flops | bytes accessed | tf_op | source)
XLA Modules:
  0.0 57.9 jit_solution(12989486218452513256)
XLA Ops:
  1.3 53.8 %shard_map.263 = (bf16[32,32,256]{2,1,0:T(8,128)(2,1)}, bf16[32,32,256]{2,1,0:T(8,128)(2,1)}, bf16[384,128]{1,0:T(8,128)(2,1)}, bf16[384,128]{1,0:T(8,128)(2,1)}, bf16[128,128]{1,0:T(8,128)(2,1)}) custom-call(s32[1]{0:T(128)S(6)} %copy.30.refs_0_, f32[32]{0:T(128)} %refs_1_.1, bf16[250,32,128]{2,1,0:T(8,128)(2,1)} %bitcast.6, bf16[250,32,128]{2,1,0:T(8,128)(2,1)} %bitcast.7, ...), custom_call_target="tpu_custom_call" | custom-call | tf_op jit(solution)/shard_map/pallas_call | solution.py:923
  55.1 2.6 %shard_map.264 = (bf16[32,32,250]{2,1,0:T(8,128)(2,1)}, f32[32,32,250]{2,1,0:T(8,128)}, f32[2,128]{1,0:T(2,128)}, f32[2,128]{1,0:T(2,128)}, f32[2,96,128]{2,1,0:...) custom-call(bf16[32,32,256]{2,1,0:T(8,128)(2,1)} %get-tuple-element., ...), custom_call_target="tpu_custom_call" | custom-call | tf_op jit(solution)/shard_map/pallas_call | solution.py:1003

commit v3 on v1

--- a/solution.py
+++ b/solution.py
@@ -318,7 +318,7 @@
         Reduction(sizes, rows, used, cuts, early_refs[l], reduction_refs[12 * l : 12 * (l + 1)])
         for l, (used, cuts, rows) in enumerate(sizes.early)
     ]
-    late = Reduction(sizes, sizes.late, sizes.late_used, (), late_ref, reduction_refs[12 * layers :])
+    late = Reduction(sizes, sizes.late, sizes.late_used, (sizes.late_vec,), late_ref, reduction_refs[12 * layers :])
 
     def head_peer(k):
         return lax.rem(me + k, heads)
@@ -757,13 +757,20 @@
                     l, width : width + 1, share * h : share * (h + 1)
                 ]
 
-    def pack_late():
-        put_norm(0, 0, 0)
-        put_qkv(0)
+    def pack_late_weights():
         for h in range(heads):
             late.out_buf[h, : 3 * hd] = g_qkv[0, 3 * hd * h : 3 * hd * (h + 1), :width].astype(
                 bf16
             )
+
+    def pack_late_vectors():
+        ones = jnp.ones((16, toks * own), bf16)
+        for h in range(heads):
+            rows = slice(3 * hd * h, 3 * hd * (h + 1))
+            grads = jnp.concatenate([gqkv_kept[w, rows] for w in everyone], axis=1)
+            vec_rows[h, 7:8, : 3 * hd] = nt(ones, grads)[:1]
+        put_norm(0, 0, 0)
+        for h in range(heads):
             late.out_buf[h, 3 * hd :] = vec_rows[h].astype(bf16)
 
     def give(w, gn, means):
@@ -815,8 +822,10 @@
             earlies[l].start_heads(1)
 
     qkv_sums(0, everyone)
-    pack_late()
+    pack_late_weights()
     late.start_heads(0)
+    pack_late_vectors()
+    late.start_heads(1)
     earlies[0].start_gather()
     batches = own // last
 
@@ -987,7 +996,7 @@
             for used, cuts, rows in sizes.early
             for ref in Reduction.scratch(sizes, rows, used, width, len(cuts) + 1)
         ]
-        + Reduction.scratch(sizes, sizes.late, sizes.late_used, width, 1),
+        + Reduction.scratch(sizes, sizes.late, sizes.late_used, width, 2),
         compiler_params=pltpu.CompilerParams(
             vmem_limit_bytes=63 * 1024 * 1024, collective_id=0, has_side_effects=True
         ),

time: 58.3 us -> 58.6 us (level)
  no operation moved by 1% of the time
where the time goes in v3:
time: 58.6 us; the launch traced here: 58.4 us
  Pallas kernels  56.9 us (97%)
  between operations  1.48 us (3%)
    pallas_call x1, Pallas kernels, exchange_pass(): pl.pallas_call(functools.partial(body, sizes), out_shape=(jax.ShapeDtypeS...  54.3 us
    pallas_call x1, Pallas kernels, finish_pass(): pl.pallas_call(functools.partial(finish_body, sizes), out_shape=(jax.Shap...  2.63 us

profile of v3, /device:TPU:0, one launch (start us, length us, event | category | flops | bytes accessed | tf_op | source)
XLA Modules:
  0.0 58.4 jit_solution(17310599810090321312)
XLA Ops:
  1.3 54.3 %shard_map.263 = (bf16[32,32,256]{2,1,0:T(8,128)(2,1)}, bf16[32,32,256]{2,1,0:T(8,128)(2,1)}, bf16[384,128]{1,0:T(8,128)(2,1)}, bf16[384,128]{1,0:T(8,128)(2,1)}, bf16[128,128]{1,0:T(8,128)(2,1)}) custom-call(s32[1]{0:T(128)S(6)} %copy.30.refs_0_, f32[32]{0:T(128)} %refs_1_.1, bf16[250,32,128]{2,1,0:T(8,128)(2,1)} %bitcast.6, bf16[250,32,128]{2,1,0:T(8,128)(2,1)} %bitcast.7, ...), custom_call_target="tpu_custom_call" | custom-call | tf_op jit(solution)/shard_map/pallas_call | solution.py:932
  55.6 2.6 %shard_map.264 = (bf16[32,32,250]{2,1,0:T(8,128)(2,1)}, f32[32,32,250]{2,1,0:T(8,128)}, f32[2,128]{1,0:T(2,128)}, f32[2,128]{1,0:T(2,128)}, f32[2,96,128]{2,1,0:...) custom-call(bf16[32,32,256]{2,1,0:T(8,128)(2,1)} %get-tuple-element., ...), custom_call_target="tpu_custom_call" | custom-call | tf_op jit(solution)/shard_map/pallas_call | solution.py:1012

commit v4 on v1

--- a/solution.py
+++ b/solution.py
@@ -507,10 +507,9 @@
         kv_all = jnp.concatenate(
             [qkv[l, w, rows_of(h, which)] for which in (1, 2) for h in range(heads)], axis=0
         )
-        made = nt(identity_tok, kv_all)
-        for r in spans(0, toks):
-            k_tok[w, r] = made[r, :width].astype(bf16)
-            v_tok[l, w, r] = made[r, width:].astype(bf16)
+        turned_kv = jnp.transpose(kv_all)
+        k_tok[w] = turned_kv[:, :width]
+        v_tok[l, w] = turned_kv[:, width:]
         for h in range(heads):
             yield
             s = nn(k_tok[w], spread_rows(qkv[l, w, rows_of(h, 0)], h, heads))

time: 58.3 us -> 57.9 us (level)
  no operation moved by 1% of the time
where the time goes in v4:
time: 57.9 us; the launch traced here: 57.7 us
  Pallas kernels  56.2 us (97%)
  between operations  1.48 us (3%)
    pallas_call x1, Pallas kernels, exchange_pass(): pl.pallas_call(functools.partial(body, sizes), out_shape=(jax.ShapeDtypeS...  53.5 us
    pallas_call x1, Pallas kernels, finish_pass(): pl.pallas_call(functools.partial(finish_body, sizes), out_shape=(jax.Shap...  2.63 us

profile of v4, /device:TPU:0, one launch (start us, length us, event | category | flops | bytes accessed | tf_op | source)
XLA Modules:
  0.0 57.7 jit_solution(985554512000092525)
XLA Ops:
  1.3 53.5 %shard_map.263 = (bf16[32,32,256]{2,1,0:T(8,128)(2,1)}, bf16[32,32,256]{2,1,0:T(8,128)(2,1)}, bf16[384,128]{1,0:T(8,128)(2,1)}, bf16[384,128]{1,0:T(8,128)(2,1)}, bf16[128,128]{1,0:T(8,128)(2,1)}) custom-call(s32[1]{0:T(128)S(6)} %copy.30.refs_0_, f32[32]{0:T(128)} %refs_1_.1, bf16[250,32,128]{2,1,0:T(8,128)(2,1)} %bitcast.6, bf16[250,32,128]{2,1,0:T(8,128)(2,1)} %bitcast.7, ...), custom_call_target="tpu_custom_call" | custom-call | tf_op jit(solution)/shard_map/pallas_call | solution.py:922
  54.8 2.6 %shard_map.264 = (bf16[32,32,250]{2,1,0:T(8,128)(2,1)}, f32[32,32,250]{2,1,0:T(8,128)}, f32[2,128]{1,0:T(2,128)}, f32[2,128]{1,0:T(2,128)}, f32[2,96,128]{2,1,0:...) custom-call(bf16[32,32,256]{2,1,0:T(8,128)(2,1)} %get-tuple-element., ...), custom_call_target="tpu_custom_call" | custom-call | tf_op jit(solution)/shard_map/pallas_call | solution.py:1002
